TPU v7x, 512 devices: a whole 4x8x8 slice. The times are simulated.
512 devices in a mesh: region: 32 (over y, z_hi), member: 16 (over x, z_lo, core).
Axes of the slice: x: 4, y: 8, z: 8 (z_hi: 4, z_lo: 2; z = z_hi * 2 + z_lo), core: 2. Of those that a mesh axis runs over, the one named last changes fastest.
Arguments:
- ensemble: bfloat16 [256, 262144], P('member', 'region'), may hold values from -6 to 6
- reports: float32 [32, 1024], P('region'), may hold values from -6 to 6
- report_count: int32 [32], P('region'), may hold values from 128 to 1024, as said below
- report_cell: int32 [32, 1024], P('region'), may hold values from 0 to 262143, as said below
- report_weight: float32 [32, 64, 1024], P('region', 'member'), may hold values from 0.001 to 1
- blending: float32 [4, 262144], P(None, ('region', 'member')), may hold values from 0.02 to 1
Outputs:
- analysis: bfloat16 [262144, 256], P(('region', 'member'))
Inputs may be any that keep to these rules, and one draw needn't show every extreme that they name: `report_count`: the largest value 1024 is reached by some region in every draw. `report_cell`: every cell lies in the slot's own region, or in the first 128 cells of one of at most two other regions chosen for that region.
All inputs are finite; a program needn't handle non-finite values.
Results may differ from a plain program's by a relative error of at most 0.0055.
Values may be sent and summed in bfloat16 or wider, within the bound.
A program may use at most 64 MiB of HBM per device.

v0:
```python
import jax
import jax.numpy as jnp
from jax import lax
from jax.sharding import PartitionSpec as P

MARGIN = 128
SWEEPS = 4
highest = lax.Precision.HIGHEST


def extended(block, sides, width):
    for axis, dim in sides:
        count = lax.axis_size(axis)
        forward = [(i, i + 1) for i in range(count - 1)]
        backward = [(target, source) for source, target in forward]
        low = lax.ppermute(
            lax.slice_in_dim(block, block.shape[dim] - width, None, axis=dim), axis, forward
        )
        high = lax.ppermute(lax.slice_in_dim(block, 0, width, axis=dim), axis, backward)
        block = jnp.concatenate([low, block, high], axis=dim)
    return block


def shifted(block, axis, distance):
    devices = range(lax.axis_size(axis))
    route = [(i - distance, i) for i in devices if i - distance in devices]
    return lax.ppermute(block, axis, route)


def make_transform(products, forcing, members):
    identity = jnp.eye(members, dtype=jnp.float32)
    precision_mat = (members - 1.0) * identity[None] + products
    frobenius = jnp.sqrt(jnp.sum(precision_mat * precision_mat, axis=(1, 2)))
    current = precision_mat / frobenius[:, None, None]
    root_iter = jnp.broadcast_to(identity, current.shape)
    for iteration in range(SWEEPS):
        middle = 1.5 * identity[None] - 0.5 * jnp.einsum(
            "aij,ajk->aik", root_iter, current, precision=highest
        )
        current = jnp.einsum("aij,ajk->aik", current, middle, precision=highest)
        root_iter = jnp.einsum("aij,ajk->aik", middle, root_iter, precision=highest)
    inverse_root = root_iter / jnp.sqrt(frobenius)[:, None, None]
    inner_step = jnp.einsum("aij,aj->ai", inverse_root, forcing, precision=highest)
    mean_weights = jnp.einsum("aij,aj->ai", inverse_root, inner_step, precision=highest)
    return (mean_weights[:, :, None] + jnp.sqrt(members - 1.0) * inverse_root).astype(jnp.bfloat16)


def corner_layout(band_index, points_here, row_count):
    group_index = jnp.arange(4 * points_here, dtype=jnp.int32)
    upper_half = group_index // (2 * points_here)
    column_block = group_index // 2 % points_here
    right_half = group_index % 2
    row_base = jnp.clip(band_index - 1 + upper_half, 0, row_count - 2)
    col_base = jnp.clip(column_block - 1 + right_half, 0, points_here - 2)
    return (row_base, col_base)


def per_device(ensemble, reports, report_count, report_cell, report_weight, blending):
    local_members, cell_count = ensemble.shape
    groups = lax.axis_size("member")
    members = local_members * groups
    region = lax.axis_index("region")
    member = lax.axis_index("member")
    targets = report_cell[0]
    holder = targets // cell_count
    within = targets % cell_count
    is_local = holder == region
    local_values = jnp.take(ensemble, jnp.where(is_local, within, 0), axis=1).astype(jnp.float32)
    border = ensemble[:, :MARGIN]
    border_index = holder * MARGIN + jnp.minimum(within, MARGIN - 1)
    pieces = lax.all_gather(border, "region", axis=1, tiled=True)
    extent = pieces.shape[1]
    inside = (border_index >= 0) & (border_index < extent) & jnp.logical_not(is_local)
    picked = jnp.take(pieces, jnp.clip(border_index, 0, extent - 1), axis=1).astype(jnp.float32)
    remote = jnp.where(inside[None, :], picked, 0.0)
    at_reports = jnp.where(is_local[None, :], local_values, remote)
    report_mean = lax.psum(jnp.sum(at_reports, axis=0), "member") / members
    local_pert = (at_reports - report_mean[None, :]).astype(jnp.bfloat16)
    report_pert = lax.all_gather(local_pert, "member", axis=0, tiled=True)
    active = (jnp.arange(report_pert.shape[1]) < report_count[0]).astype(jnp.float32)
    weights = report_weight[0] * active[None, :]
    weighted = (report_pert[None, :, :] * weights[:, None, :]).astype(jnp.bfloat16)
    departure = (weights * (reports[0] - report_mean)[None, :]).astype(jnp.bfloat16)
    products = jnp.einsum("ako,jo->akj", weighted, report_pert, preferred_element_type=jnp.float32)
    forcing = jnp.einsum("ao,ko->ak", departure, report_pert, preferred_element_type=jnp.float32)
    transform = make_transform(products, forcing, members)
    points_here = transform.shape[0]
    groups_band = 4 * points_here
    slab_cells = cell_count // groups
    group_cells = slab_cells // groups_band
    mixing = blending / jnp.sum(blending, axis=0, keepdims=True)
    everyone = lax.all_gather(ensemble, "member", axis=0, tiled=True)
    region_mean = jnp.sum(everyone, axis=0, dtype=jnp.float32) / members
    anomaly = (everyone - region_mean[None, :]).astype(jnp.bfloat16)
    near_mix = extended(mixing, (("member", 1),), slab_cells)
    totals = []
    for offset_band in range(3):
        band_index = member - 1 + offset_band
        slab_start = jnp.clip(band_index, 0, groups - 1) * slab_cells
        slab_anomaly = lax.dynamic_slice_in_dim(anomaly, slab_start, slab_cells, 1)
        slab_anomaly = slab_anomaly.reshape(members, groups_band, group_cells)
        mix_part = near_mix[:, offset_band * slab_cells : (offset_band + 1) * slab_cells]
        mix_part = mix_part.reshape(4, groups_band, group_cells)
        row_base, col_base = corner_layout(band_index, points_here, groups)
        row_step = (member - row_base)[:, None]
        running = jnp.zeros((groups_band, group_cells, members), jnp.float32)
        for col_step in range(2):
            weight = jnp.where(
                row_step == 0,
                mix_part[col_step],
                jnp.where(row_step == 1, mix_part[2 + col_step], 0.0),
            )
            chosen = jnp.take(transform, col_base + col_step, axis=0)
            spread = jnp.einsum(
                "kgc,gkj->gcj", slab_anomaly, chosen, preferred_element_type=jnp.float32
            )
            running = running + weight[:, :, None] * spread
        totals.append(running.reshape(slab_cells, members))
    from_below = shifted(totals[2], "member", 1)
    from_above = shifted(totals[0].astype(jnp.bfloat16), "member", -1).astype(jnp.float32)
    blended = totals[1] + from_below + from_above
    cell_mean = lax.dynamic_slice_in_dim(region_mean, member * slab_cells, slab_cells, 0)
    return (cell_mean[:, None] + blended).astype(jnp.bfloat16)


def solution(mesh):
    return jax.shard_map(
        per_device,
        mesh=mesh,
        in_specs=(
            P("member", "region"),
            P("region", None),
            P("region"),
            P("region", None),
            P("region", "member", None),
            P(None, ("region", "member")),
        ),
        out_specs=P(("region", "member"), None),
        check_vma=False,
    )
```

profile of v0, /device:TPU:1, one launch (start us, length us, event | category | flops | bytes accessed | tf_op | source)
XLA Modules:
  0.0 213.5 jit_solution(11608834173221068432)
XLA Ops:
  8.0 8.8 %collective-permute-start = (f32[4,512]{1,0:T(4,128)S(1)}, f32[4,512]{1,0:T(4,128)S(1)}, u32[]{:S(2)}, u32[]{:S(2)}) collective-permute-start(f32[4,512]{1,0:T(4,128)S(1)} %broadcast_divide_fusion.3), channel_id=1, source_target_pairs={{1,0},{2,1},{3,2},{4,3},{5,4},{6,5},{7,6},{8,7},{9,8},{10,9},{11,1... | collective-permute-start | bytes 24584 | tf_op jit(solution)/shard_map/ppermute | solution.py:19
  16.8 1.9 collective-permute-start.2
  18.7 1.9 copy.15
  20.8 3.2 %gather_fusion = bf16[1024,16]{1,0:T(8,128)(2,1)S(1)} fusion(bf16[16,8192]{0,1:T(8,128)(2,1)S(1)} %copy.15, s32[1024]{0:T(1024)S(1)} %broadcast_clamp_fusion.1), kind=kCustom, calls=%fused_computation.2 | custom fusion | bytes 69632 | tf_op jit(solution)/shard_map/jit(_take)/gather | solution.py:68
  24.1 76.4 %all_gather.10 = bf16[16,4096]{0,1:T(8,128)(2,1)S(1)} all-gather(bf16[16,128]{0,1:T(8,128)(2,1)S(1)} %slice.74), channel_id=1, replica_groups=mesh['region'=32,'member'=16] {'region'}, dimensions={1}, use_global_device_ids=true | all-gather | bytes 135168 | tf_op jit(solution)/shard_map/all_gather | solution.py:71
  100.5 3.2 %gather_fusion.1 = bf16[1024,16]{1,0:T(8,128)(2,1)S(1)} fusion(bf16[16,4096]{0,1:T(8,128)(2,1)S(1)} %all_gather.10, s32[1024]{0:T(1024)S(1)} %broadcast_clamp_fusion), kind=kCustom, calls=%fused_computation.3 | custom fusion | bytes 69632 | tf_op jit(solution)/shard_map/jit(_take)/gather | solution.py:74
  103.9 41.0 %psum.7 = f32[1024]{0:T(1024)S(1)} all-reduce(f32[1024]{0:T(1024)S(1)} %fusion.21), channel_id=1, replica_groups=mesh['region'=32,'member'=16] {'member'}, use_global_device_ids=true, to_apply=%region_3.4 | all-reduce | flops 1024 | bytes 8192 | tf_op jit(solution)/shard_map/psum | solution.py:77
  145.6 19.1 %all_gather.11 = bf16[256,1024]{1,0:T(8,128)(2,1)S(1)} all-gather(bf16[16,1024]{1,0:T(8,128)(2,1)S(1)} %fusion.22), channel_id=1, replica_groups=mesh['region'=32,'member'=16] {'member'}, dimensions={0}, use_global_device_ids=true | all-gather | bytes 557056 | tf_op jit(solution)/shard_map/all_gather | solution.py:79
  165.1 0.9 multiply_reduce_fusion
  166.0 1.2 fusion.8
  167.2 1.1 fusion.14
  168.3 1.2 fusion.20
  169.5 1.2 fusion.7
  170.7 1.1 fusion.42
  171.9 1.1 fusion.43
  173.0 1.2 fusion.6
  174.2 1.1 fusion.44
  175.4 1.1 fusion.45
  176.5 1.4 fusion.5
  177.9 1.1 convolution_divide_fusion
  179.0 1.0 fusion.28
  180.0 1.0 fusion.26
  182.5 2.0 gather_fusion.2
  185.4 3.0 %convert_reduce_fusion = f32[8192]{0:T(1024)S(1)} fusion(bf16[256,8192]{1,0:T(8,128)(2,1)} %all-gather.2.cloned.1.call-done), kind=kLoop, calls=%fused_computation.5 | loop fusion | flops 4186112 | bytes 4227072 | tf_op jit(solution)/shard_map/reduce_sum | solution.py:93
  188.8 0.9 fusion
  190.5 1.1 copy-done.1
  191.6 1.3 multiply_add_fusion
  192.9 2.8 %collective-permute-start.1 = (f32[512,256]{1,0:T(8,128)}, f32[512,256]{1,0:T(8,128)S(1)}, u32[]{:S(2)}, u32[]{:S(2)}) collective-permute-start(f32[512,256]{1,0:T(8,128)} %bitcast.16), channel_id=1, source_target_pairs={{0,1},{1,2},{2,3},{3,4},{4,5},{5,6},{6,7},{7,8},{8,9},{9,10},{10,1... | collective-permute-start | bytes 1572872 | tf_op jit(solution)/shard_map/ppermute | solution.py:27
  196.6 1.1 copy-done.2
  198.2 1.9 collective-permute-start.3
  201.2 4.6 %collective-permute-done.3 = bf16[512,256]{1,0:T(8,128)(2,1)S(1)} collective-permute-done((bf16[512,256]{1,0:T(8,128)(2,1)S(1)}, bf16[512,256]{1,0:T(8,128)(2,1)S(1)}, u32[]{:S(2)}, u32[]{:S(2)}) %collective-permute-start.3) | collective-permute-done | bytes 262176 | tf_op jit(solution)/shard_map/ppermute | solution.py:27
  205.9 0.8 fusion.12
  (80 shorter events, 8.2 us)
Async XLA Ops:
  6.5 14.1 %copy-start.3 = (s32[1,1024]{1,0:T(1,128)S(1)}, s32[1,1024]{1,0:T(1,128)}, u32[]{:S(2)}) copy-start(s32[1,1024]{1,0:T(1,128)} %param.11) | copy-start | bytes 12292
  6.5 178.8 %all-gather.2.cloned.1.call-start = ((), (), s32[]{:S(2)}) async-start(), calls=%async_computation | async-start | bytes 4456448 | tf_op jit(solution)/shard_map/all_gather | solution.py:92
  8.0 176.6 %collective-permute-start = (f32[4,512]{1,0:T(4,128)S(1)}, f32[4,512]{1,0:T(4,128)S(1)}, u32[]{:S(2)}, u32[]{:S(2)}) collective-permute-start(f32[4,512]{1,0:T(4,128)S(1)} %broadcast_divide_fusion.3), channel_id=1, source_target_pairs={{1,0},{2,1},{3,2},{4,3},{5,4},{6,5},{7,6},{8,7},{9,8},{10,9},{11,1... | collective-permute-start | bytes 24584 | tf_op jit(solution)/shard_map/ppermute | solution.py:19
  16.8 168.1 %collective-permute-start.2 = (f32[4,512]{1,0:T(4,128)S(1)}, f32[4,512]{1,0:T(4,128)S(1)}, u32[]{:S(2)}, u32[]{:S(2)}) collective-permute-start(f32[4,512]{1,0:T(4,128)S(1)} %broadcast_divide_fusion.3), channel_id=1, source_target_pairs={{0,1},{1,2},{2,3},{3,4},{4,5},{5,6},{6,7},{7,8},{8,9},{9,10},{10,1... | collective-permute-start | bytes 24584 | tf_op jit(solution)/shard_map/ppermute | solution.py:16
  18.7 126.2 %copy-start.5 = (f32[1,1024]{1,0:T(1,128)S(1)}, f32[1,1024]{1,0:T(1,128)}, u32[]{:S(2)}) copy-start(f32[1,1024]{1,0:T(1,128)} %param.9) | copy-start | bytes 12292
  100.5 64.4 %copy-start.4 = (f32[1,4,1024]{2,1,0:T(4,128)S(1)}, f32[1,4,1024]{2,1,0:T(4,128)}, u32[]{:S(2)}) copy-start(f32[1,4,1024]{2,1,0:T(4,128)} %param.12) | copy-start | bytes 49156
  185.4 3.5 %copy-start = (bf16[256,8192]{1,0:T(8,128)(2,1)S(1)}, bf16[256,8192]{1,0:T(8,128)(2,1)}, u32[]{:S(2)}) copy-start(bf16[256,8192]{1,0:T(8,128)(2,1)} %all-gather.2.cloned.1.call-done) | copy-start | bytes 12582916
  190.0 1.6 copy-start.1
  192.9 12.9 %collective-permute-start.1 = (f32[512,256]{1,0:T(8,128)}, f32[512,256]{1,0:T(8,128)S(1)}, u32[]{:S(2)}, u32[]{:S(2)}) collective-permute-start(f32[512,256]{1,0:T(8,128)} %bitcast.16), channel_id=1, source_target_pairs={{0,1},{1,2},{2,3},{3,4},{4,5},{5,6},{6,7},{7,8},{8,9},{9,10},{10,1... | collective-permute-start | bytes 1572872 | tf_op jit(solution)/shard_map/ppermute | solution.py:27
  196.0 1.6 copy-start.2
  198.2 7.7 %collective-permute-start.3 = (bf16[512,256]{1,0:T(8,128)(2,1)S(1)}, bf16[512,256]{1,0:T(8,128)(2,1)S(1)}, u32[]{:S(2)}, u32[]{:S(2)}) collective-permute-start(bf16[512,256]{1,0:T(8,128)(2,1)S(1)} %bitcast.89), channel_id=1, source_target_pairs={{1,0},{2,1},{3,2},{4,3},{5,4},{6,5},{7,6},{8,7},{9,8},{10,9},{11,1... | collective-permute-start | bytes 786440 | tf_op jit(solution)/shard_map/ppermute | solution.py:27
Sparse Core Ops, SparseCore 0:
  18.8 47.7 all-gather.1
where the time goes:
time: 214 us
  blocking collectives  136 us (64%)
  matrix products  19.9 us (9%)
  local copies, waits for them, and re-layouts  15.4 us (7%)
  starting transfers between devices  15.4 us (7%)
  between operations  14.5 us (7%)
  other arithmetic  7.2 us (3%)
  waiting for transfers between devices  4.65 us (2%)
    all_gather x1, blocking collectives, per_device(): pieces = lax.all_gather(border, 'region', axis=1, tiled=True)  76.4 us
    psum x1, blocking collectives, per_device(): report_mean = lax.psum(jnp.sum(at_reports, axis=0), 'member') / members  41 us
    all_gather x1, blocking collectives, per_device(): report_pert = lax.all_gather(local_pert, 'member', axis=0, tiled=True)  19.1 us
    ppermute x1, starting transfers between devices, extended(): lax.ppermute(lax.slice_in_dim(block, 0, width, axis=dim), axis, backward)  8.78 us
    dot_general x4, matrix products, make_transform(): jnp.einsum('aij,ajk->aik', root_iter, current, precision=highest)  4.9 us
    ppermute x2, starting transfers between devices, shifted(): return lax.ppermute(block, axis, route)  4.74 us
    ppermute x2, waiting for transfers between devices, shifted(): return lax.ppermute(block, axis, route)  4.63 us
    dot_general x4, matrix products, make_transform(): root_iter = jnp.einsum('aij,ajk->aik', middle, root_iter, precision=highest)  4.53 us
  transfers between devices with their start and end apart: 5, of which 1 were waited for; matrix products, arithmetic and copies ran while one was open for 15% of the time, Pallas kernels for 0%

commit v1 on v0

--- a/solution.py
+++ b/solution.py
@@ -74,7 +74,7 @@
     picked = jnp.take(pieces, jnp.clip(border_index, 0, extent - 1), axis=1).astype(jnp.float32)
     remote = jnp.where(inside[None, :], picked, 0.0)
     at_reports = jnp.where(is_local[None, :], local_values, remote)
-    report_mean = lax.psum(jnp.sum(at_reports, axis=0), "member") / members
+    report_mean = jnp.sum(lax.all_gather(jnp.sum(at_reports, axis=0), "member"), axis=0) / members
     local_pert = (at_reports - report_mean[None, :]).astype(jnp.bfloat16)
     report_pert = lax.all_gather(local_pert, "member", axis=0, tiled=True)
     active = (jnp.arange(report_pert.shape[1]) < report_count[0]).astype(jnp.float32)

time: 214 us -> 206 us (0.963)
  blocking collectives: 136 us -> 128 us
    psum x1 -> x0, blocking collectives: 41 us -> none  [per_device(): report_mean = lax.psum(jnp.sum(at_reports, axis=0), 'member') / members]
    all_gather x0 -> x1, blocking collectives: none -> 33.1 us  [per_device(): lax.all_gather(jnp.sum(at_reports, axis=0), 'member')]
where the time goes in v1:
time: 206 us; the launch traced here: 205 us
  blocking collectives  128 us (62%)
  matrix products  19.9 us (10%)
  starting transfers between devices  15.7 us (8%)
  local copies, waits for them, and re-layouts  15.4 us (7%)
  between operations  14.6 us (7%)
  other arithmetic  7.23 us (4%)
  waiting for transfers between devices  4.65 us (2%)
    all_gather x1, blocking collectives, per_device(): pieces = lax.all_gather(border, 'region', axis=1, tiled=True)  76.3 us
    all_gather x1, blocking collectives, per_device(): lax.all_gather(jnp.sum(at_reports, axis=0), 'member')  33.1 us
    all_gather x1, blocking collectives, per_device(): report_pert = lax.all_gather(local_pert, 'member', axis=0, tiled=True)  18.6 us
    ppermute x1, starting transfers between devices, extended(): lax.ppermute(lax.slice_in_dim(block, 0, width, axis=dim), axis, backward)  8.78 us
    ppermute x2, starting transfers between devices, shifted(): return lax.ppermute(block, axis, route)  5.01 us
    dot_general x4, matrix products, make_transform(): jnp.einsum('aij,ajk->aik', root_iter, current, precision=highest)  4.91 us
    ppermute x2, waiting for transfers between devices, shifted(): return lax.ppermute(block, axis, route)  4.63 us
    dot_general x4, matrix products, make_transform(): root_iter = jnp.einsum('aij,ajk->aik', middle, root_iter, precision=highest)  4.53 us
  transfers between devices with their start and end apart: 5, of which 1 were waited for; matrix products, arithmetic and copies ran while one was open for 15% of the time, Pallas kernels for 0%

profile of v1, /device:TPU:1, one launch (start us, length us, event | category | flops | bytes accessed | tf_op | source)
XLA Modules:
  0.0 205.4 jit_solution(6713759882962123731)
XLA Ops:
  8.0 8.8 %collective-permute-start = (f32[4,512]{1,0:T(4,128)S(1)}, f32[4,512]{1,0:T(4,128)S(1)}, u32[]{:S(2)}, u32[]{:S(2)}) collective-permute-start(f32[4,512]{1,0:T(4,128)S(1)} %broadcast_divide_fusion.3), channel_id=1, source_target_pairs={{1,0},{2,1},{3,2},{4,3},{5,4},{6,5},{7,6},{8,7},{9,8},{10,9},{11,1... | collective-permute-start | bytes 24584 | tf_op jit(solution)/shard_map/ppermute | solution.py:19
  16.8 1.9 collective-permute-start.2
  18.7 1.9 copy.29
  20.8 3.2 %gather_fusion = bf16[1024,16]{1,0:T(8,128)(2,1)S(1)} fusion(bf16[16,8192]{0,1:T(8,128)(2,1)S(1)} %copy.29, s32[1024]{0:T(1024)S(1)} %broadcast_clamp_fusion.1), kind=kCustom, calls=%fused_computation.2 | custom fusion | bytes 69632 | tf_op jit(solution)/shard_map/jit(_take)/gather | solution.py:68
  24.1 76.3 %all_gather.16 = bf16[16,4096]{0,1:T(8,128)(2,1)S(1)} all-gather(bf16[16,128]{0,1:T(8,128)(2,1)S(1)} %slice.74), channel_id=1, replica_groups=mesh['region'=32,'member'=16] {'region'}, dimensions={1}, use_global_device_ids=true | all-gather | bytes 135168 | tf_op jit(solution)/shard_map/all_gather | solution.py:71
  100.4 3.2 %gather_fusion.1 = bf16[1024,16]{1,0:T(8,128)(2,1)S(1)} fusion(bf16[16,4096]{0,1:T(8,128)(2,1)S(1)} %all_gather.16, s32[1024]{0:T(1024)S(1)} %broadcast_clamp_fusion), kind=kCustom, calls=%fused_computation.3 | custom fusion | bytes 69632 | tf_op jit(solution)/shard_map/jit(_take)/gather | solution.py:74
  103.8 33.1 %all-gather = f32[16384]{0:T(1024)S(1)} all-gather(f32[1024]{0:T(1024)S(1)} %fusion.21), channel_id=2, replica_groups=mesh['region'=32,'member'=16] {'member'}, dimensions={0}, use_global_device_ids=true | all-gather | bytes 69632 | tf_op jit(solution)/shard_map/all_gather | solution.py:77
  137.7 18.6 %all_gather.19 = bf16[256,1024]{1,0:T(8,128)(2,1)S(1)} all-gather(bf16[16,1024]{1,0:T(8,128)(2,1)S(1)} %fusion.22), channel_id=1, replica_groups=mesh['region'=32,'member'=16] {'member'}, dimensions={0}, use_global_device_ids=true | all-gather | bytes 557056 | tf_op jit(solution)/shard_map/all_gather | solution.py:79
  156.8 0.9 multiply_reduce_fusion
  157.7 1.2 fusion.8
  158.8 1.1 fusion.14
  159.9 1.2 fusion.20
  161.1 1.2 fusion.7
  162.3 1.1 fusion.41
  163.5 1.1 fusion.42
  164.6 1.2 fusion.6
  165.8 1.1 fusion.43
  167.0 1.1 fusion.44
  168.2 1.4 fusion.5
  169.5 1.1 convolution_divide_fusion
  170.7 1.0 fusion.28
  171.7 1.0 fusion.26
  174.1 2.0 gather_fusion.2
  177.0 3.0 %convert_reduce_fusion = f32[8192]{0:T(1024)S(1)} fusion(bf16[256,8192]{1,0:T(8,128)(2,1)} %all-gather.3.cloned.1.call-done), kind=kLoop, calls=%fused_computation.5 | loop fusion | flops 4186112 | bytes 4227072 | tf_op jit(solution)/shard_map/reduce_sum | solution.py:93
  180.5 0.9 fusion
  182.2 1.1 copy-done.1
  183.2 1.3 multiply_add_fusion
  184.6 3.1 %collective-permute-start.1 = (f32[512,256]{1,0:T(8,128)}, f32[512,256]{1,0:T(8,128)S(1)}, u32[]{:S(2)}, u32[]{:S(2)}) collective-permute-start(f32[512,256]{1,0:T(8,128)} %bitcast.17), channel_id=1, source_target_pairs={{0,1},{1,2},{2,3},{3,4},{4,5},{5,6},{6,7},{7,8},{8,9},{9,10},{10,1... | collective-permute-start | bytes 1572872 | tf_op jit(solution)/shard_map/ppermute | solution.py:27
  188.5 1.1 copy-done.2
  190.1 1.9 collective-permute-start.3
  193.1 4.6 %collective-permute-done.3 = bf16[512,256]{1,0:T(8,128)(2,1)S(1)} collective-permute-done((bf16[512,256]{1,0:T(8,128)(2,1)S(1)}, bf16[512,256]{1,0:T(8,128)(2,1)S(1)}, u32[]{:S(2)}, u32[]{:S(2)}) %collective-permute-start.3) | collective-permute-done | bytes 262176 | tf_op jit(solution)/shard_map/ppermute | solution.py:27
  197.8 0.8 fusion.12
  (83 shorter events, 8.2 us)
Async XLA Ops:
  6.5 14.1 %copy-start.3 = (s32[1,1024]{1,0:T(1,128)S(1)}, s32[1,1024]{1,0:T(1,128)}, u32[]{:S(2)}) copy-start(s32[1,1024]{1,0:T(1,128)} %param.11) | copy-start | bytes 12292
  6.5 170.5 %all-gather.3.cloned.1.call-start = ((), (), s32[]{:S(2)}) async-start(), calls=%async_computation | async-start | bytes 4456448 | tf_op jit(solution)/shard_map/all_gather | solution.py:92
  8.0 168.2 %collective-permute-start = (f32[4,512]{1,0:T(4,128)S(1)}, f32[4,512]{1,0:T(4,128)S(1)}, u32[]{:S(2)}, u32[]{:S(2)}) collective-permute-start(f32[4,512]{1,0:T(4,128)S(1)} %broadcast_divide_fusion.3), channel_id=1, source_target_pairs={{1,0},{2,1},{3,2},{4,3},{5,4},{6,5},{7,6},{8,7},{9,8},{10,9},{11,1... | collective-permute-start | bytes 24584 | tf_op jit(solution)/shard_map/ppermute | solution.py:19
  16.8 159.8 %collective-permute-start.2 = (f32[4,512]{1,0:T(4,128)S(1)}, f32[4,512]{1,0:T(4,128)S(1)}, u32[]{:S(2)}, u32[]{:S(2)}) collective-permute-start(f32[4,512]{1,0:T(4,128)S(1)} %broadcast_divide_fusion.3), channel_id=1, source_target_pairs={{0,1},{1,2},{2,3},{3,4},{4,5},{5,6},{6,7},{7,8},{8,9},{9,10},{10,1... | collective-permute-start | bytes 24584 | tf_op jit(solution)/shard_map/ppermute | solution.py:16
  24.1 132.3 %copy-start.5 = (f32[1,1024]{1,0:T(1,128)S(1)}, f32[1,1024]{1,0:T(1,128)}, u32[]{:S(2)}) copy-start(f32[1,1024]{1,0:T(1,128)} %param.9) | copy-start | bytes 12292
  100.4 56.1 %copy-start.4 = (f32[1,4,1024]{2,1,0:T(4,128)S(1)}, f32[1,4,1024]{2,1,0:T(4,128)}, u32[]{:S(2)}) copy-start(f32[1,4,1024]{2,1,0:T(4,128)} %param.12) | copy-start | bytes 49156
  177.0 3.5 %copy-start = (bf16[256,8192]{1,0:T(8,128)(2,1)S(1)}, bf16[256,8192]{1,0:T(8,128)(2,1)}, u32[]{:S(2)}) copy-start(bf16[256,8192]{1,0:T(8,128)(2,1)} %all-gather.3.cloned.1.call-done) | copy-start | bytes 12582916
  181.6 1.6 copy-start.1
  184.6 13.2 %collective-permute-start.1 = (f32[512,256]{1,0:T(8,128)}, f32[512,256]{1,0:T(8,128)S(1)}, u32[]{:S(2)}, u32[]{:S(2)}) collective-permute-start(f32[512,256]{1,0:T(8,128)} %bitcast.17), channel_id=1, source_target_pairs={{0,1},{1,2},{2,3},{3,4},{4,5},{5,6},{6,7},{7,8},{8,9},{9,10},{10,1... | collective-permute-start | bytes 1572872 | tf_op jit(solution)/shard_map/ppermute | solution.py:27
  187.9 1.6 copy-start.2
  190.1 7.7 %collective-permute-start.3 = (bf16[512,256]{1,0:T(8,128)(2,1)S(1)}, bf16[512,256]{1,0:T(8,128)(2,1)S(1)}, u32[]{:S(2)}, u32[]{:S(2)}) collective-permute-start(bf16[512,256]{1,0:T(8,128)(2,1)S(1)} %bitcast.91), channel_id=1, source_target_pairs={{1,0},{2,1},{3,2},{4,3},{5,4},{6,5},{7,6},{8,7},{9,8},{10,9},{11,1... | collective-permute-start | bytes 786440 | tf_op jit(solution)/shard_map/ppermute | solution.py:27
Sparse Core Ops, SparseCore 0:
  18.8 47.7 all-gather.2
